TPU v7x, 256 devices: a whole 4x4x8 slice. The times are simulated.
256 devices in a mesh: seq: 16 (over z, core), chan: 16 (over x, y).
Axes of the slice: x: 4, y: 4, z: 8, core: 2. Of those that a mesh axis runs over, the one named last changes fastest.
Arguments:
- grad_out: bfloat16 [8192, 8192], P('seq', 'chan'), may hold values from -6 to 6
- qkv_saved: bfloat16 [8192, 3, 8192], P('seq', None, 'chan'), may hold values from -6 to 6
- conv_saved: bfloat16 [8192, 8192], P('seq', 'chan'), may hold values from -6 to 6
- long_taps: bfloat16 [8192, 512], P('seq', 'chan'), may hold values from -1 to 1
- short_taps: float32 [3, 3, 8192], P(None, None, 'chan'), may hold values from -3 to 3
Outputs:
- grad_proj: bfloat16 [8192, 3, 8192], P(('seq', 'chan'))
All inputs are finite; a program needn't handle non-finite values.
Results may differ from a plain program's by a relative error of at most 0.0042.
Values may be sent and summed in bfloat16 or wider, within the bound.
A program may use at most 64 MiB of HBM per device.

v0:
```python
import jax
import jax.numpy as jnp
from jax import lax
from jax.sharding import PartitionSpec as P

tile_rows = 128


def shifted(value, axis, steps):
    count = lax.axis_size(axis)
    leading, last = (max(0, -steps), min(count, count - steps))
    return lax.ppermute(value, axis, [(source, source + steps) for source in range(leading, last)])


def band_matrix(window):
    groups = window.shape[0]
    rolled = jnp.concatenate(
        [
            window[:, tile_rows - 1 :],
            jnp.zeros((groups, 1), window.dtype),
            window[:, : tile_rows - 1],
        ],
        1,
    )
    spread = jnp.broadcast_to(rolled[:, None, :], (groups, tile_rows, 2 * tile_rows))
    flat = spread.reshape(groups, 2 * tile_rows * tile_rows)[:, : tile_rows * (2 * tile_rows - 1)]
    return flat.reshape(groups, tile_rows, 2 * tile_rows - 1)[:, :, :tile_rows]


def correlate(gradients, filters, first_row, out_rows, span):
    groups = gradients.shape[0]
    per_group = gradients.shape[1]
    tiles_out = out_rows // tile_rows
    padded_grads = jnp.concatenate(
        [gradients, jnp.zeros((groups, per_group, out_rows), gradients.dtype)], 2
    )
    padded_taps = jnp.concatenate(
        [
            jnp.zeros((groups, tile_rows), filters.dtype),
            filters,
            jnp.zeros((groups, tile_rows), filters.dtype),
        ],
        1,
    )

    def advance(offset, running):
        lag_start = offset * tile_rows
        window = lax.dynamic_slice_in_dim(padded_taps, lag_start + 1, 2 * tile_rows - 1, 1)
        band = band_matrix(window)
        source = lax.dynamic_slice_in_dim(padded_grads, first_row + lag_start, out_rows, 2)
        source = source.reshape(groups, per_group * tiles_out, tile_rows)
        product = lax.dot_general(
            source, band, (((2,), (2,)), ((0,), (0,))), preferred_element_type=jnp.float32
        )
        return running + product

    start = jnp.zeros((groups, per_group * tiles_out, tile_rows), jnp.float32)
    summed = lax.fori_loop(0, span // tile_rows, advance, start)
    return summed.reshape(groups * per_group, out_rows)


def on_device(grad_out, qkv_saved, conv_saved, long_taps, short_taps):
    block_rows = grad_out.shape[0]
    channels = grad_out.shape[1]
    shards = lax.axis_size("seq")
    position = lax.axis_index("seq")
    total_rows = shards * block_rows
    out_wide = grad_out.astype(jnp.float32)
    query = qkv_saved[:, 0, :]
    key_part = qkv_saved[:, 1, :]
    value_part = qkv_saved[:, 2, :]
    grad_query = out_wide * conv_saved.astype(jnp.float32)
    grad_mixed = (out_wide * query.astype(jnp.float32)).astype(jnp.bfloat16)
    mixed_lanes = grad_mixed.T
    taps_lanes = long_taps.T
    local_groups = long_taps.shape[1]
    per_group = channels // local_groups
    all_grads, all_filters = (
        lax.all_gather(mixed_lanes, "seq", axis=1, tiled=True),
        lax.all_gather(taps_lanes, "seq", axis=1, tiled=True),
    )
    shaped = all_grads.reshape(local_groups, per_group, total_rows)
    first_row = position * block_rows
    grad_lanes = correlate(shaped, all_filters, first_row, block_rows, total_rows - first_row)
    grad_z = grad_lanes.T
    grad_key = grad_z * value_part.astype(jnp.float32)
    grad_value = grad_z * key_part.astype(jnp.float32)
    stacked = jnp.stack([grad_query, grad_key, grad_value], 1)
    short_len = short_taps.shape[1]
    borrowed = shifted(stacked[: short_len - 1], "seq", -1)
    extended = jnp.concatenate([stacked, borrowed], 0)
    result = jnp.zeros_like(stacked)
    for lag_index in range(short_len):
        result = (
            result
            + short_taps[:, lag_index, :][None] * extended[lag_index : lag_index + block_rows]
        )
    mixed = result.astype(jnp.bfloat16)
    return lax.all_to_all(mixed, "chan", split_axis=0, concat_axis=2, tiled=True)


def solution(mesh):
    in_specs = (
        P("seq", "chan"),
        P("seq", None, "chan"),
        P("seq", "chan"),
        P("seq", "chan"),
        P(None, None, "chan"),
    )
    out_specs = P(("seq", "chan"), None, None)
    return jax.shard_map(
        on_device, mesh=mesh, in_specs=in_specs, out_specs=out_specs, check_vma=False
    )
```

profile of v0, /device:TPU:1, one launch (start us, length us, event | category | flops | bytes accessed | tf_op | source)
XLA Modules:
  0.0 1056.2 jit_solution(16561877445356904248)
XLA Ops:
  12.3 24.1 %all_gather.7 = bf16[32,8192]{1,0:T(8,128)(2,1)S(1)} all-gather(bf16[32,512]{1,0:T(8,128)(2,1)S(1)} %bitcast.53), channel_id=1, replica_groups=mesh['seq'=16,'chan'=16] {'seq'}, dimensions={1}, use_global_device_ids=true | all-gather | bytes 557056 | tf_op jit(solution)/shard_map/all_gather | solution.py:80
  37.2 34.3 %all-gather.2.cloned.1.call-done = bf16[512,8192]{1,0:T(8,128)(2,1)} async-done(((bf16[512,512]{1,0:T(8,128)(2,1)}), bf16[512,8192]{1,0:T(8,128)(2,1)}) %all-gather.2.cloned.1.call-update) | async-done | bytes 8388624 | tf_op jit(solution)/shard_map/all_gather | solution.py:79
  79.2 858.0 %while.12 = (s32[]{:T(128)}, f32[32,64,128]{2,1,0:T(8,128)S(1)}, s32[]{:T(128)}, s32[]{:T(128)}, bf16[32,16,8704]{2,1,0:T(8,128)(2,1)}, /*index=5*/bf16[32,8448]...) while((s32[]{:T(128)}, f32[32,64,128]{2,1,0:T(8,128)S(1)}, ...), condition=%wide.region_1.2_spmd, body=%wide.region_0.1_spmd.sunk | while | flops 67420168 | bytes 20497480 | solution.py:58
  96.6 7.8 reshape.43
  110.9 7.8 reshape.43
  125.2 7.8 reshape.43
  139.5 7.8 reshape.43
  153.8 7.8 reshape.43
  168.1 7.8 reshape.43
  182.4 7.8 reshape.43
  196.7 7.8 reshape.43
  211.0 7.8 reshape.43
  225.3 7.8 reshape.43
  239.7 7.8 reshape.43
  253.9 7.8 reshape.43
  268.2 7.8 reshape.43
  282.5 7.8 reshape.43
  296.8 7.8 reshape.43
  311.1 7.8 reshape.43
  325.4 7.8 reshape.43
  354.0 7.8 reshape.43
  368.3 7.8 reshape.43
  382.6 7.8 reshape.43
  396.9 7.8 reshape.43
  411.2 7.8 reshape.43
  425.5 7.8 reshape.43
  439.8 7.8 reshape.43
  454.1 7.8 reshape.43
  468.4 7.8 reshape.43
  482.7 7.8 reshape.43
  942.9 59.4 %collective-permute-start = (f32[2,3,512]{2,0,1:T(2,128)S(1)}, f32[2,3,512]{2,0,1:T(2,128)S(1)}, u32[]{:S(2)}, u32[]{:S(2)}) collective-permute-start(f32[2,3,512]{2,0,1:T(2,128)S(1)} %copy.27), channel_id=1, source_target_pairs={{16,0},{32,16},{48,32},{64,48},{80,64},{96,80},{112,96},{128,112},... | collective-permute-start | bytes 36872 | tf_op jit(solution)/shard_map/ppermute | solution.py:12
  1012.6 33.5 %all_to_all.18 = bf16[512,3,512]{2,1,0:T(4,128)(2,1)S(1)} all-to-all(bf16[512,3,512]{2,1,0:T(4,128)(2,1)S(1)} %copy.29), channel_id=1, replica_groups=mesh['seq'=16,'chan'=16] {'chan'}, dimensions={0} | all-to-all | bytes 3145728 | tf_op jit(solution)/shard_map/all_to_all | solution.py:99
  (671 shorter events, 678.2 us)
Async XLA Ops:
  6.5 1.8 copy-start.1
  6.5 2.0 copy-start.2
  6.5 65.0 %all-gather.2.cloned.1.call-start = ((), (), s32[]{:S(2)}) async-start(), calls=%async_computation.1 | async-start | bytes 8912896 | tf_op jit(solution)/shard_map/all_gather | solution.py:79
  8.8 3.5 copy-start.4
  8.8 3.5 copy-start.3
  937.3 3.0 copy-start
  942.9 60.2 %collective-permute-start = (f32[2,3,512]{2,0,1:T(2,128)S(1)}, f32[2,3,512]{2,0,1:T(2,128)S(1)}, u32[]{:S(2)}, u32[]{:S(2)}) collective-permute-start(f32[2,3,512]{2,0,1:T(2,128)S(1)} %copy.27), channel_id=1, source_target_pairs={{16,0},{32,16},{48,32},{64,48},{80,64},{96,80},{112,96},{128,112},... | collective-permute-start | bytes 36872 | tf_op jit(solution)/shard_map/ppermute | solution.py:12
Sparse Core Ops, SparseCore 0:
  10.3 61.1 all-gather.1
where the time goes:
time: 1070 us; the launch traced here: 1060 us
  local copies, waits for them, and re-layouts  750 us (70%)
  matrix products  123 us (11%)
  starting transfers between devices  59.4 us (6%)
  blocking collectives  57.6 us (5%)
  waiting for transfers between devices  35.1 us (3%)
  other arithmetic  14.1 us (1%)
  between operations  13.6 us (1%)
    reshape x60, local copies, waits for them, and re-layouts, band_matrix(): return flat.reshape(groups, tile_rows, 2 * tile_rows - 1)[:, :, :tile_rows]  465 us
    dot_general x60, matrix products, advance(): lax.dot_general(source, band, (((2,), (2,)), ((0,), (0,))), preferred_ele...  123 us
    while x60, local copies, waits for them, and re-layouts  72.3 us
    dynamic_slice x60, local copies, waits for them, and re-layouts, advance(): lax.dynamic_slice_in_dim(padded_grads, first_row + lag_start, out_rows, 2)  64.5 us
    ppermute x1, starting transfers between devices, shifted(): lax.ppermute(value, axis, [(source, source + steps) for source in range(l...  59.4 us
    slice x60, local copies, waits for them, and re-layouts, band_matrix(): window[:, :tile_rows - 1]  46.3 us
    slice x60, local copies, waits for them, and re-layouts, band_matrix(): window[:, tile_rows - 1:]  42.2 us
    all_gather x1, waiting for transfers between devices, on_device(): lax.all_gather(mixed_lanes, 'seq', axis=1, tiled=True)  34.3 us
  transfers between devices with their start and end apart: 2, of which 2 were waited for; matrix products, arithmetic and copies ran while one was open for 0% of the time, Pallas kernels for 0%

commit v1 on v0

v1 whole, which is shorter than its diff:
```python
import functools

import jax
import jax.numpy as jnp
from jax import lax
from jax.experimental import pallas as pl
from jax.experimental.pallas import tpu as pltpu
from jax.sharding import PartitionSpec as P

MESH = pl.DeviceIdType.MESH
f32 = jnp.float32
bf16 = jnp.bfloat16

LANES = 128
TILE = 256
PER = 16
SEG = 8


def kernel(
    S, C,
    go_ref, qkv_ref, cv_ref, tp_ref, st_ref, out_ref,
    tap_send, tap_recv, rev_ref, strip, x_send, x_recv, acc, y_send, y_recv,
    eq, ez, wq, wz,
    tap_sem, x_ssem, x_rsem, y_ssem, y_rsem, h_ssem, h_rsem, o_ssem, o_rsem,
):
    rows, channels = go_ref.shape
    half = channels // 2
    tiles = S * rows // TILE
    own = rows // TILE
    part = rows // C
    me_s = lax.axis_index("seq")
    me_c = lax.axis_index("chan")

    def local(src, dst, sem):
        pltpu.make_async_copy(src, dst, sem).start()

    def landed(ref, sem):
        pltpu.make_async_copy(ref, ref, sem).wait()

    def seq_copy(src, dst, ssem, rsem, j):
        return pltpu.make_async_remote_copy(
            src_ref=src, dst_ref=dst, send_sem=ssem, recv_sem=rsem,
            device_id=(j, me_c), device_id_type=MESH,
        )

    def chan_copy(src, dst, ssem, rsem, j):
        return pltpu.make_async_remote_copy(
            src_ref=src, dst_ref=dst, send_sem=ssem, recv_sem=rsem,
            device_id=(me_s, j), device_id_type=MESH,
        )

    barrier = pltpu.get_barrier_semaphore()

    def greet_seq(k, carry):
        pl.semaphore_signal(barrier, inc=1, device_id=(lax.rem(me_s + k, S), me_c), device_id_type=MESH)
        return carry

    def greet_chan(k, carry):
        pl.semaphore_signal(barrier, inc=1, device_id=(me_s, lax.rem(me_c + k, C)), device_id_type=MESH)
        return carry

    lax.fori_loop(1, S, greet_seq, 0)
    lax.fori_loop(1, C, greet_chan, 0)

    quarters = rows // LANES
    for g in range(2):
        for q in range(quarters):
            tap_send[:, g * quarters + q, :] = tp_ref[g * S:(g + 1) * S, q * LANES:(q + 1) * LANES].astype(f32)

    def mix(g):
        cols = slice(g * half, (g + 1) * half)
        gm = (go_ref[:, cols].astype(f32) * qkv_ref[0, :, cols].astype(f32)).astype(bf16)
        turned = gm.T
        for h in range(own):
            x_send[g, :, h] = turned[:, h * TILE:(h + 1) * TILE].reshape(S, PER, TILE)

    mix(0)
    pl.semaphore_wait(barrier, S + C - 2)

    local(tap_send.at[me_s], tap_recv.at[me_s], tap_sem.at[1])

    def push_taps(k, carry):
        j = lax.rem(me_s + k, S)
        seq_copy(tap_send.at[j], tap_recv.at[me_s], tap_sem.at[0], tap_sem.at[1], j).start()
        return carry

    lax.fori_loop(1, S, push_taps, 0)

    def push_x(g):
        mine = pl.ds(me_s * own, own)
        local(x_send.at[g, me_s], x_recv.at[g, mine], x_rsem.at[g])

        def push(k, carry):
            j = lax.rem(me_s + k, S)
            seq_copy(x_send.at[g, j], x_recv.at[g, mine], x_ssem.at[g], x_rsem.at[g], j).start()
            return carry

        lax.fori_loop(1, S, push, 0)

    push_x(0)
    mix(1)
    push_x(1)

    def halo(src, dst, n):
        return seq_copy(src, dst, h_ssem.at[n], h_rsem.at[n], lax.rem(me_s + S - 1, S))

    def push_halo(src, dst, n):
        @pl.when(me_s > 0)
        def _():
            halo(src, dst, n).start()

        @pl.when(me_s == S - 1)
        def _():
            dst[...] = jnp.zeros(dst.shape, dst.dtype)

    def wait_halo(src, dst, n):
        @pl.when(me_s < S - 1)
        def _():
            halo(src, dst, n).wait_recv()

    def wait_halo_sent(src, dst, n):
        @pl.when(me_s > 0)
        def _():
            halo(src, dst, n).wait_send()

    def taps3(e, first, taps):
        block = e[pl.ds(first, part + 8), :]
        return taps[0:1] * block[0:part] + taps[1:2] * block[1:part + 1] + taps[2:3] * block[2:part + 2]

    def chan_chunks(body):
        def step(k, carry):
            body(lax.rem(me_c + k, C - 1))
            return carry

        lax.fori_loop(0, C - 1, step, 0)

    eq[0:rows, :] = go_ref[...].astype(f32) * cv_ref[...].astype(f32)
    q_src, q_dst = eq.at[0:8, :], eq.at[rows:rows + 8, :]
    push_halo(q_src, q_dst, 0)

    def query_chunk(c):
        first = pl.multiple_of(c * part, part)
        at = pl.ds(first, part)
        wq[at, :] = taps3(eq, first, st_ref[0]).astype(bf16)
        dst = out_ref.at[0, :, pl.ds(pl.multiple_of(me_c * channels, channels), channels)]

        @pl.when(c == me_c)
        def _():
            local(wq.at[at, :], dst, o_rsem.at[2])

        @pl.when(c != me_c)
        def _():
            chan_copy(wq.at[at, :], dst, o_ssem.at[2], o_rsem.at[2], c).start()

    chan_chunks(query_chunk)
    wait_halo(q_src, q_dst, 0)
    query_chunk(C - 1)

    landed(tap_recv, tap_sem.at[1])
    down = lax.broadcasted_iota(jnp.int32, (LANES, LANES), 0)
    over = lax.broadcasted_iota(jnp.int32, (LANES, LANES), 1)
    mirror = (lax.rem(down + over, LANES) == 0).astype(f32).astype(bf16)
    rev = jnp.dot(
        tap_recv[...].reshape(S * 2 * quarters, LANES).astype(bf16), mirror, preferred_element_type=f32
    )
    rev_ref[...] = rev.reshape(S, 2, quarters, LANES)
    newer = (over == 0) | (over >= LANES - down)

    def grow(s, before):
        after = []
        for g in range(2):
            last = before[g]
            for q in range(quarters):
                row = rev_ref[s, g, q:q + 1, :]
                mixed = jnp.where(newer, jnp.broadcast_to(row, (LANES, LANES)), jnp.broadcast_to(last, (LANES, LANES)))
                rolled = pltpu.roll(mixed, 0, 1, stride=1, stride_axis=0)
                at = pl.multiple_of((s * quarters + q + 1) * LANES, LANES)
                strip[g, pl.ds(at, LANES), :] = rolled.astype(bf16)
                last = row
            after.append(last)
        return tuple(after)

    strip[:, 0:LANES, :] = jnp.zeros((2, LANES, LANES), bf16)
    nothing = jnp.zeros((1, LANES), f32)
    lax.fori_loop(0, S, grow, (nothing, nothing))

    for g in range(2):
        x_recv[g, tiles:tiles + SEG - 1] = jnp.zeros((SEG - 1, PER, TILE), bf16)

    def correlate(g):
        landed(x_recv.at[g, 0:tiles], x_rsem.at[g])
        for seg in range(tiles // SEG):
            n = tiles - seg * SEG
            deep = SEG * TILE
            left = jnp.concatenate(
                [x_recv[g, seg * SEG + d:seg * SEG + d + n].reshape(n * PER, TILE) for d in range(SEG)], 1
            )
            right = jnp.concatenate(
                [
                    strip[g, LANES + seg * deep:LANES + (seg + 1) * deep, :],
                    strip[g, seg * deep:(seg + 1) * deep, :],
                ],
                1,
            )
            product = jnp.dot(left, right, preferred_element_type=f32)
            if seg == 0:
                acc[...] = product
            else:
                acc[0:n * PER, :] += product
        y_send[g] = acc[...].astype(bf16).reshape(tiles, PER, TILE)
        local(y_send.at[g, pl.ds(me_s * own, own)], y_recv.at[g, me_s], y_rsem.at[g])

        def push(k, carry):
            j = lax.rem(me_s + k, S)
            seq_copy(
                y_send.at[g, pl.ds(j * own, own)], y_recv.at[g, me_s], y_ssem.at[g], y_rsem.at[g], j
            ).start()
            return carry

        lax.fori_loop(1, S, push, 0)

    correlate(0)
    correlate(1)

    def finish(g):
        cols = slice(g * half, (g + 1) * half)
        landed(y_recv.at[g], y_rsem.at[g])
        for h in range(own):
            at = slice(h * TILE, (h + 1) * TILE)
            gz = y_recv[g, :, h].reshape(half, TILE).T.astype(f32)
            ez[g, 0, at, :] = gz * qkv_ref[2, at, cols].astype(f32)
            ez[g, 1, at, :] = gz * qkv_ref[1, at, cols].astype(f32)
        src, dst = ez.at[g, :, 0:8, :], ez.at[g, :, rows:rows + 8, :]
        push_halo(src, dst, 1 + g)

        def chunk(c):
            first = pl.multiple_of(c * part, part)
            at = pl.ds(first, part)
            for p in range(2):
                wz[g, p, at, :] = taps3(ez.at[g, p], first, st_ref[1 + p, :, cols]).astype(bf16)
            block = wz.at[g, :, at, :]
            to = out_ref.at[1:3, :, pl.ds(pl.multiple_of(me_c * channels + g * half, half), half)]

            @pl.when(c == me_c)
            def _():
                local(block, to, o_rsem.at[g])

            @pl.when(c != me_c)
            def _():
                chan_copy(block, to, o_ssem.at[g], o_rsem.at[g], c).start()

        chan_chunks(chunk)
        wait_halo(src, dst, 1 + g)
        chunk(C - 1)

    finish(0)
    finish(1)

    landed(out_ref.at[0], o_rsem.at[2])
    for g in range(2):
        landed(out_ref.at[1:3, :, 0:C * half], o_rsem.at[g])

    landed(tap_send.at[0:S - 1], tap_sem.at[0])
    landed(wq.at[0:rows - part, :], o_ssem.at[2])
    wait_halo_sent(q_src, q_dst, 0)
    for g in range(2):
        landed(x_send.at[g, 0:S - 1], x_ssem.at[g])
        landed(y_send.at[g, 0:tiles - own], y_ssem.at[g])
        landed(wz.at[g, :, 0:rows - part, :], o_ssem.at[g])
        wait_halo_sent(ez.at[g, :, 0:8, :], ez.at[g, :, rows:rows + 8, :], 1 + g)


def on_device(S, C, grad_out, qkv_saved, conv_saved, long_taps, short_taps):
    rows, channels = grad_out.shape
    half = channels // 2
    tiles = S * rows // TILE
    own = rows // TILE
    quarters = rows // LANES
    vmem = pl.BlockSpec(memory_space=pltpu.VMEM)
    out = pl.pallas_call(
        functools.partial(kernel, S, C),
        out_shape=jax.ShapeDtypeStruct((3, rows // C, C * channels), bf16),
        in_specs=[vmem] * 5,
        out_specs=pl.BlockSpec(memory_space=pl.ANY),
        scratch_shapes=[
            pltpu.VMEM((S, 2 * quarters, LANES), f32),
            pltpu.VMEM((S, 2 * quarters, LANES), f32),
            pltpu.VMEM((S, 2, quarters, LANES), f32),
            pltpu.VMEM((2, LANES + tiles * TILE, LANES), bf16),
            pltpu.VMEM((2, S, own, PER, TILE), bf16),
            pltpu.VMEM((2, tiles + SEG, PER, TILE), bf16),
            pltpu.VMEM((tiles * PER, TILE), f32),
            pltpu.VMEM((2, tiles, PER, TILE), bf16),
            pltpu.VMEM((2, S, own, PER, TILE), bf16),
            pltpu.VMEM((rows + 8, channels), f32),
            pltpu.VMEM((2, 2, rows + 8, half), f32),
            pltpu.VMEM((rows, channels), bf16),
            pltpu.VMEM((2, 2, rows, half), bf16),
            pltpu.SemaphoreType.DMA((2,)),
            pltpu.SemaphoreType.DMA((2,)),
            pltpu.SemaphoreType.DMA((2,)),
            pltpu.SemaphoreType.DMA((2,)),
            pltpu.SemaphoreType.DMA((2,)),
            pltpu.SemaphoreType.DMA((3,)),
            pltpu.SemaphoreType.DMA((3,)),
            pltpu.SemaphoreType.DMA((3,)),
            pltpu.SemaphoreType.DMA((3,)),
        ],
        compiler_params=pltpu.CompilerParams(
            collective_id=0, has_side_effects=True, vmem_limit_bytes=48 * 1024 * 1024
        ),
    )(grad_out, qkv_saved.transpose(1, 0, 2), conv_saved, long_taps.T, short_taps)
    return out.transpose(1, 0, 2)


def solution(mesh):
    in_specs = (
        P("seq", "chan"),
        P("seq", None, "chan"),
        P("seq", "chan"),
        P("seq", "chan"),
        P(None, None, "chan"),
    )
    out_specs = P(("seq", "chan"), None, None)
    return jax.shard_map(
        functools.partial(on_device, mesh.shape["seq"], mesh.shape["chan"]),
        mesh=mesh, in_specs=in_specs, out_specs=out_specs, check_vma=False,
    )
```

time: 1070 us -> 58.5 us (0.05); the launches traced: 1060 us -> 58.2 us
  local copies, waits for them, and re-layouts: 750 us -> 6.13 us
  matrix products: 123 us -> 0 us
  starting transfers between devices: 59.4 us -> 0 us
  blocking collectives: 57.6 us -> 0 us
  Pallas kernels: 0 us -> 52.1 us
  waiting for transfers between devices: 35.1 us -> 0 us
  other arithmetic: 14.1 us -> 0 us
  between operations: 13.6 us -> 0.01 us
    reshape x121 -> x0, local copies, waits for them, and re-layouts: 485 us -> none  [the longest x60 465 us: band_matrix(): return flat.reshape(groups, tile_rows, 2 * tile_rows - 1)[:, :, :tile_rows]]
    dot_general x60 -> x0, matrix products: 123 us -> none  [advance(): lax.dot_general(source, band, (((2,), (2,)), ((0,), (0,))), preferred_ele...]
    slice x184 -> x0, local copies, waits for them, and re-layouts: 101 us -> none  [the longest x60 46.3 us: band_matrix(): window[:, :tile_rows - 1]]
    while x60 -> x0, local copies, waits for them, and re-layouts: 72.3 us -> none
    dynamic_slice x60 -> x0, local copies, waits for them, and re-layouts: 64.5 us -> none  [advance(): lax.dynamic_slice_in_dim(padded_grads, first_row + lag_start, out_rows, 2)]
    ppermute x1 -> x0, starting transfers between devices: 59.4 us -> none  [shifted(): lax.ppermute(value, axis, [(source, source + steps) for source in range(l...]
    pallas_call x0 -> x1, Pallas kernels: none -> 52.1 us  [on_device(): pl.pallas_call(functools.partial(kernel, S, C), out_shape=jax.ShapeDtypeS...]
    all_gather x1 -> x0, waiting for transfers between devices: 34.3 us -> none  [on_device(): lax.all_gather(mixed_lanes, 'seq', axis=1, tiled=True)]
  transfers between devices with their start and end apart: 2 -> 0, of which waited for: 2 -> 0; matrix products, arithmetic and copies ran while one was open for 0% -> 0% of each run, Pallas kernels for 0% -> 0%
where the time goes in v1:
time: 58.5 us; the launch traced here: 58.2 us
  Pallas kernels  52.1 us (89%)
  local copies, waits for them, and re-layouts  6.13 us (10%)
    pallas_call x1, Pallas kernels, on_device(): pl.pallas_call(functools.partial(kernel, S, C), out_shape=jax.ShapeDtypeS...  52.1 us
    unnamed x11, local copies, waits for them, and re-layouts  6.13 us

profile of v1, /device:TPU:1, one launch (start us, length us, event | category | flops | bytes accessed | tf_op | source)
XLA Modules:
  0.0 58.2 jit_solution(1603461175980530582)
XLA Ops:
  0.0 0.0 copy-start
  0.0 1.4 %copy-done = bf16[512,3,512]{2,0,1:T(8,128)(2,1)S(1)} copy-done((bf16[512,3,512]{2,0,1:T(8,128)(2,1)S(1)}, bf16[512,3,512]{2,0,1:T(8,128)(2,1)}, u32[]{:S(2)}) %copy-start) | copy-done | bytes 1572888
  1.4 0.0 copy-start.1
  1.4 1.0 %copy-done.1 = bf16[512,512]{1,0:T(8,128)(2,1)S(1)} copy-done((bf16[512,512]{1,0:T(8,128)(2,1)S(1)}, bf16[512,512]{1,0:T(8,128)(2,1)}, u32[]{:S(2)}) %copy-start.1) | copy-done | bytes 524312
  2.5 0.0 copy-start.2
  2.5 1.0 %copy-done.2 = bf16[512,512]{1,0:T(8,128)(2,1)S(1)} copy-done((bf16[512,512]{1,0:T(8,128)(2,1)S(1)}, bf16[512,512]{1,0:T(8,128)(2,1)}, u32[]{:S(2)}) %copy-start.2) | copy-done | bytes 524312
  3.5 0.0 copy-start.3
  3.5 0.8 %copy-done.3 = bf16[512,32]{0,1:T(8,128)(2,1)S(1)} copy-done((bf16[512,32]{0,1:T(8,128)(2,1)S(1)}, bf16[512,32]{0,1:T(8,128)(2,1)}, u32[]{:S(2)}) %copy-start.3) | copy-done | bytes 32792
  4.3 0.0 copy-start.4
  4.3 0.7 %copy-done.4 = f32[3,3,512]{2,1,0:T(4,128)S(1)} copy-done((f32[3,3,512]{2,1,0:T(4,128)S(1)}, f32[3,3,512]{2,1,0:T(4,128)}, u32[]{:S(2)}) %copy-start.4) | copy-done | bytes 18456
  5.0 52.1 %shard_map.55 = bf16[3,32,8192]{2,1,0:T(8,128)(2,1)S(1)} custom-call(bf16[512,512]{1,0:T(8,128)(2,1)S(1)} %copy-done.1, bf16[3,512,512]{2,1,0:T(8,128)(2,1)S(1)} %bitcast.4, bf16[512,512]{1,0:T(8,128)(2,1)S(1)} %copy-done.2, bf16[32,512]{1,0:T(8,128)(2,1)S(1)} %bitcast.5, f32[3,3,512]{2,1,0:T(4,128)S(1)} %copy-done.4), custom_call_target="tpu_custom_call" | custom-call | tf_op jit(solution)/shard_map/pallas_call | solution.py:281
  57.1 1.1 %copy.7 = bf16[32,3,8192]{2,0,1:T(8,128)(2,1)} copy(bf16[32,3,8192]{2,0,1:T(8,128)(2,1)S(1)} %bitcast.3) | data formatting | bytes 3145728
Async XLA Ops:
  0.0 1.4 %copy-start = (bf16[512,3,512]{2,0,1:T(8,128)(2,1)S(1)}, bf16[512,3,512]{2,0,1:T(8,128)(2,1)}, u32[]{:S(2)}) copy-start(bf16[512,3,512]{2,0,1:T(8,128)(2,1)} %param.6) | copy-start | bytes 4718596
  1.4 1.0 %copy-start.1 = (bf16[512,512]{1,0:T(8,128)(2,1)S(1)}, bf16[512,512]{1,0:T(8,128)(2,1)}, u32[]{:S(2)}) copy-start(bf16[512,512]{1,0:T(8,128)(2,1)} %go_ref.1) | copy-start | bytes 1572868
  2.5 1.0 %copy-start.2 = (bf16[512,512]{1,0:T(8,128)(2,1)S(1)}, bf16[512,512]{1,0:T(8,128)(2,1)}, u32[]{:S(2)}) copy-start(bf16[512,512]{1,0:T(8,128)(2,1)} %cv_ref.1) | copy-start | bytes 1572868
  3.5 0.8 %copy-start.3 = (bf16[512,32]{0,1:T(8,128)(2,1)S(1)}, bf16[512,32]{0,1:T(8,128)(2,1)}, u32[]{:S(2)}) copy-start(bf16[512,32]{0,1:T(8,128)(2,1)} %param.8) | copy-start | bytes 98308
  4.3 0.7 %copy-start.4 = (f32[3,3,512]{2,1,0:T(4,128)S(1)}, f32[3,3,512]{2,1,0:T(4,128)}, u32[]{:S(2)}) copy-start(f32[3,3,512]{2,1,0:T(4,128)} %st_ref.1) | copy-start | bytes 55300

commit v2 on v1

--- a/solution.py
+++ b/solution.py
@@ -1,4 +1,5 @@
 import functools
+import math
 
 import jax
 import jax.numpy as jnp
@@ -19,7 +20,8 @@
 
 def kernel(
     S, C,
-    go_ref, qkv_ref, cv_ref, tp_ref, st_ref, out_ref,
+    go_hbm, qkv_hbm, cv_hbm, tp_hbm, st_hbm, out_ref,
+    go_ref, qkv_ref, cv_ref, tp_ref, st_ref, in_sem,
     tap_send, tap_recv, rev_ref, strip, x_send, x_recv, acc, y_send, y_recv,
     eq, ez, wq, wz,
     tap_sem, x_ssem, x_rsem, y_ssem, y_rsem, h_ssem, h_rsem, o_ssem, o_rsem,
@@ -50,6 +52,44 @@
             device_id=(me_s, j), device_id_type=MESH,
         )
 
+    turn = 1 - 2 * lax.rem(me_s, 2)
+    if S % 2 == 0:
+        chips = S // 2
+        steps = sorted(range(1, chips), key=lambda z: -min(z, chips - z))
+        seq_order = [
+            lax.rem(me_s // 2 + turn * z + chips, chips) * 2 + lax.rem(me_s + core, 2) for z in steps for core in range(2)
+        ] + [me_s + turn]
+    else:
+        seq_order = [lax.rem(me_s + k, S) for k in range(1, S)]
+    side = math.isqrt(C)
+    if side * side == C:
+        moves = sorted(
+            [(x, y) for x in range(side) for y in range(side) if x + y > 0],
+            key=lambda m: -(min(m[0], side - m[0]) + min(m[1], side - m[1])),
+        )
+        chan_order = [
+            lax.rem(me_c // side + turn * x + side, side) * side + lax.rem(lax.rem(me_c, side) + turn * y + side, side)
+            for x, y in moves
+        ]
+    else:
+        chan_order = [lax.rem(me_c + k, C) for k in range(1, C)]
+
+    loads = {}
+
+    def load(name, src, dst):
+        loads[name] = pltpu.make_async_copy(src, dst, in_sem.at[len(loads)])
+        loads[name].start()
+
+    for g in range(2):
+        cols = slice(g * half, (g + 1) * half)
+        load(f"go{g}", go_hbm.at[:, cols], go_ref.at[:, cols])
+        load(f"q{g}", qkv_hbm.at[0, :, cols], qkv_ref.at[0, :, cols])
+        if g == 0:
+            load("tp", tp_hbm, tp_ref)
+    load("cv", cv_hbm, cv_ref)
+    load("st", st_hbm, st_ref)
+    load("kv", qkv_hbm.at[1:3], qkv_ref.at[1:3])
+
     barrier = pltpu.get_barrier_semaphore()
 
     def greet_seq(k, carry):
@@ -64,12 +104,15 @@
     lax.fori_loop(1, C, greet_chan, 0)
 
     quarters = rows // LANES
+    loads["tp"].wait()
     for g in range(2):
         for q in range(quarters):
             tap_send[:, g * quarters + q, :] = tp_ref[g * S:(g + 1) * S, q * LANES:(q + 1) * LANES].astype(f32)
 
     def mix(g):
         cols = slice(g * half, (g + 1) * half)
+        loads[f"go{g}"].wait()
+        loads[f"q{g}"].wait()
         gm = (go_ref[:, cols].astype(f32) * qkv_ref[0, :, cols].astype(f32)).astype(bf16)
         turned = gm.T
         for h in range(own):
@@ -80,23 +123,15 @@
 
     local(tap_send.at[me_s], tap_recv.at[me_s], tap_sem.at[1])
 
-    def push_taps(k, carry):
-        j = lax.rem(me_s + k, S)
+    for j in seq_order:
         seq_copy(tap_send.at[j], tap_recv.at[me_s], tap_sem.at[0], tap_sem.at[1], j).start()
-        return carry
-
-    lax.fori_loop(1, S, push_taps, 0)
 
     def push_x(g):
         mine = pl.ds(me_s * own, own)
         local(x_send.at[g, me_s], x_recv.at[g, mine], x_rsem.at[g])
 
-        def push(k, carry):
-            j = lax.rem(me_s + k, S)
+        for j in seq_order:
             seq_copy(x_send.at[g, j], x_recv.at[g, mine], x_ssem.at[g], x_rsem.at[g], j).start()
-            return carry
-
-        lax.fori_loop(1, S, push, 0)
 
     push_x(0)
     mix(1)
@@ -125,37 +160,46 @@
             halo(src, dst, n).wait_send()
 
     def taps3(e, first, taps):
-        block = e[pl.ds(first, part + 8), :]
-        return taps[0:1] * block[0:part] + taps[1:2] * block[1:part + 1] + taps[2:3] * block[2:part + 2]
-
-    def chan_chunks(body):
-        def step(k, carry):
-            body(lax.rem(me_c + k, C - 1))
-            return carry
-
-        lax.fori_loop(0, C - 1, step, 0)
-
+        return sum(taps[j:j + 1] * e[first + j:first + j + part, :] for j in range(3))
+
+    def spread(source, dst, ssem, rsem, blocks):
+        def send(c):
+            block = source(pl.ds(pl.multiple_of(c * part, part), part))
+
+            @pl.when(c == me_c)
+            def _():
+                local(block, dst, rsem)
+
+            @pl.when(c != me_c)
+            def _():
+                chan_copy(block, dst, ssem, rsem, c).start()
+
+        if blocks == "last":
+            send(C - 1)
+            return
+        for c in chan_order:
+
+            @pl.when(c < C - 1)
+            def _(c=c):
+                chan_copy(source(pl.ds(pl.multiple_of(c * part, part), part)), dst, ssem, rsem, c).start()
+
+        @pl.when(me_c < C - 1)
+        def _():
+            local(source(pl.ds(pl.multiple_of(me_c * part, part), part)), dst, rsem)
+
+    loads["cv"].wait()
+    loads["st"].wait()
     eq[0:rows, :] = go_ref[...].astype(f32) * cv_ref[...].astype(f32)
     q_src, q_dst = eq.at[0:8, :], eq.at[rows:rows + 8, :]
     push_halo(q_src, q_dst, 0)
 
-    def query_chunk(c):
-        first = pl.multiple_of(c * part, part)
-        at = pl.ds(first, part)
-        wq[at, :] = taps3(eq, first, st_ref[0]).astype(bf16)
+    def query(blocks):
+        for c in range(C - 1) if blocks == "first" else [C - 1]:
+            wq[c * part:(c + 1) * part, :] = taps3(eq, c * part, st_ref[0]).astype(bf16)
         dst = out_ref.at[0, :, pl.ds(pl.multiple_of(me_c * channels, channels), channels)]
-
-        @pl.when(c == me_c)
-        def _():
-            local(wq.at[at, :], dst, o_rsem.at[2])
-
-        @pl.when(c != me_c)
-        def _():
-            chan_copy(wq.at[at, :], dst, o_ssem.at[2], o_rsem.at[2], c).start()
-
-    chan_chunks(query_chunk)
-    wait_halo(q_src, q_dst, 0)
-    query_chunk(C - 1)
+        spread(lambda at: wq.at[at, :], dst, o_ssem.at[2], o_rsem.at[2], blocks)
+
+    query("first")
 
     landed(tap_recv, tap_sem.at[1])
     down = lax.broadcasted_iota(jnp.int32, (LANES, LANES), 0)
@@ -211,17 +255,28 @@
         y_send[g] = acc[...].astype(bf16).reshape(tiles, PER, TILE)
         local(y_send.at[g, pl.ds(me_s * own, own)], y_recv.at[g, me_s], y_rsem.at[g])
 
-        def push(k, carry):
-            j = lax.rem(me_s + k, S)
+        for j in seq_order:
             seq_copy(
                 y_send.at[g, pl.ds(j * own, own)], y_recv.at[g, me_s], y_ssem.at[g], y_rsem.at[g], j
             ).start()
-            return carry
-
-        lax.fori_loop(1, S, push, 0)
 
     correlate(0)
+    wait_halo(q_src, q_dst, 0)
+    query("last")
     correlate(1)
+
+    def weigh(g, blocks):
+        cols = slice(g * half, (g + 1) * half)
+        for c in range(C - 1) if blocks == "first" else [C - 1]:
+            for p in range(2):
+                wz[g, p, c * part:(c + 1) * part, :] = taps3(
+                    ez.at[g, p], c * part, st_ref[1 + p, :, cols]
+                ).astype(bf16)
+        dst = out_ref.at[1:3, :, pl.ds(pl.multiple_of(me_c * channels + g * half, half), half)]
+        spread(lambda at: wz.at[g, :, at, :], dst, o_ssem.at[g], o_rsem.at[g], blocks)
+
+    def halo_ends(g):
+        return ez.at[g, :, 0:8, :], ez.at[g, :, rows:rows + 8, :]
 
     def finish(g):
         cols = slice(g * half, (g + 1) * half)
@@ -231,31 +286,16 @@
             gz = y_recv[g, :, h].reshape(half, TILE).T.astype(f32)
             ez[g, 0, at, :] = gz * qkv_ref[2, at, cols].astype(f32)
             ez[g, 1, at, :] = gz * qkv_ref[1, at, cols].astype(f32)
-        src, dst = ez.at[g, :, 0:8, :], ez.at[g, :, rows:rows + 8, :]
-        push_halo(src, dst, 1 + g)
-
-        def chunk(c):
-            first = pl.multiple_of(c * part, part)
-            at = pl.ds(first, part)
-            for p in range(2):
-                wz[g, p, at, :] = taps3(ez.at[g, p], first, st_ref[1 + p, :, cols]).astype(bf16)
-            block = wz.at[g, :, at, :]
-            to = out_ref.at[1:3, :, pl.ds(pl.multiple_of(me_c * channels + g * half, half), half)]
-
-            @pl.when(c == me_c)
-            def _():
-                local(block, to, o_rsem.at[g])
-
-            @pl.when(c != me_c)
-            def _():
-                chan_copy(block, to, o_ssem.at[g], o_rsem.at[g], c).start()
-
-        chan_chunks(chunk)
-        wait_halo(src, dst, 1 + g)
-        chunk(C - 1)
-
+            if h == 0:
+                push_halo(*halo_ends(g), 1 + g)
+        weigh(g, "first")
+
+    loads["kv"].wait()
     finish(0)
     finish(1)
+    for g in range(2):
+        wait_halo(*halo_ends(g), 1 + g)
+        weigh(g, "last")
 
     landed(out_ref.at[0], o_rsem.at[2])
     for g in range(2):
@@ -268,7 +308,7 @@
         landed(x_send.at[g, 0:S - 1], x_ssem.at[g])
         landed(y_send.at[g, 0:tiles - own], y_ssem.at[g])
         landed(wz.at[g, :, 0:rows - part, :], o_ssem.at[g])
-        wait_halo_sent(ez.at[g, :, 0:8, :], ez.at[g, :, rows:rows + 8, :], 1 + g)
+        wait_halo_sent(*halo_ends(g), 1 + g)
 
 
 def on_device(S, C, grad_out, qkv_saved, conv_saved, long_taps, short_taps):
@@ -277,13 +317,18 @@
     tiles = S * rows // TILE
     own = rows // TILE
     quarters = rows // LANES
-    vmem = pl.BlockSpec(memory_space=pltpu.VMEM)
     out = pl.pallas_call(
         functools.partial(kernel, S, C),
         out_shape=jax.ShapeDtypeStruct((3, rows // C, C * channels), bf16),
-        in_specs=[vmem] * 5,
+        in_specs=[pl.BlockSpec(memory_space=pltpu.HBM)] * 5,
         out_specs=pl.BlockSpec(memory_space=pl.ANY),
         scratch_shapes=[
+            pltpu.VMEM((rows, channels), bf16),
+            pltpu.VMEM((3, rows, channels), bf16),
+            pltpu.VMEM((rows, channels), bf16),
+            pltpu.VMEM((2 * S, rows), bf16),
+            pltpu.VMEM((3, 3, channels), f32),
+            pltpu.SemaphoreType.DMA((8,)),
             pltpu.VMEM((S, 2 * quarters, LANES), f32),
             pltpu.VMEM((S, 2 * quarters, LANES), f32),
             pltpu.VMEM((S, 2, quarters, LANES), f32),
@@ -310,7 +355,10 @@
         compiler_params=pltpu.CompilerParams(
             collective_id=0, has_side_effects=True, vmem_limit_bytes=48 * 1024 * 1024
         ),
-    )(grad_out, qkv_saved.transpose(1, 0, 2), conv_saved, long_taps.T, short_taps)
+    )(*[
+        pltpu.with_memory_space_constraint(value, pltpu.HBM)
+        for value in (grad_out, qkv_saved.transpose(1, 0, 2), conv_saved, long_taps.T, short_taps)
+    ])
     return out.transpose(1, 0, 2)
 
 

time: 58.5 us -> 51.3 us (0.88)
  the two profiles are of different devices: /device:TPU:1 before, /device:TPU:30 now
where the time goes in v2:
time: 51.3 us; the launch traced here: 51.2 us
  Pallas kernels  50.1 us (98%)
  local copies, waits for them, and re-layouts  1.15 us (2%)
    pallas_call x1, Pallas kernels, on_device(): pl.pallas_call(functools.partial(kernel, S, C), out_shape=jax.ShapeDtypeS...  50.1 us
    unnamed x1, local copies, waits for them, and re-layouts  1.15 us

profile of v2, /device:TPU:30, one launch (start us, length us, event | category | flops | bytes accessed | tf_op | source)
XLA Modules:
  0.0 51.2 jit_solution(2501069790588163176)
XLA Ops:
  0.0 50.1 %shard_map.55 = bf16[3,32,8192]{2,1,0:T(8,128)(2,1)S(1)} custom-call(bf16[512,512]{1,0:T(8,128)(2,1)} %go_hbm.1, bf16[3,512,512]{2,1,0:T(8,128)(2,1)} %bitcast.4, bf16[512,512]{1,0:T(8,128)(2,1)} %cv_hbm.1, bf16[32,512]{1,0:T(8,128)(2,1)} %bitcast.5, f32[3,3,512]{2,1,0:T(4,128)} %st_hbm.1), custom_call_target="tpu_custom_call" | custom-call | tf_op jit(solution)/shard_map/pallas_call | solution.py:320
  50.1 1.1 %copy.7 = bf16[32,3,8192]{2,0,1:T(8,128)(2,1)} copy(bf16[32,3,8192]{2,0,1:T(8,128)(2,1)S(1)} %bitcast.3) | data formatting | bytes 3145728

commit v3 on v2

--- a/solution.py
+++ b/solution.py
@@ -23,8 +23,8 @@
     go_hbm, qkv_hbm, cv_hbm, tp_hbm, st_hbm, out_ref,
     go_ref, qkv_ref, cv_ref, tp_ref, st_ref, in_sem,
     tap_send, tap_recv, rev_ref, strip, x_send, x_recv, acc, y_send, y_recv,
-    eq, ez, wq, wz,
-    tap_sem, x_ssem, x_rsem, y_ssem, y_rsem, h_ssem, h_rsem, o_ssem, o_rsem,
+    edge_send, edge_recv, kv_edge, eq, ez, wq, wz,
+    tap_sem, x_ssem, x_rsem, y_ssem, y_rsem, e_ssem, e_rsem, h_ssem, h_rsem, o_ssem, o_rsem,
 ):
     rows, channels = go_ref.shape
     half = channels // 2
@@ -137,6 +137,12 @@
     mix(1)
     push_x(1)
 
+    loads["kv"].wait()
+    kv_copy = seq_copy(
+        qkv_ref.at[1:3, 0:PER, :], kv_edge, h_ssem.at[1], h_rsem.at[1], lax.rem(me_s + S - 1, S)
+    )
+    kv_copy.start()
+
     def halo(src, dst, n):
         return seq_copy(src, dst, h_ssem.at[n], h_rsem.at[n], lax.rem(me_s + S - 1, S))
 
@@ -162,30 +168,22 @@
     def taps3(e, first, taps):
         return sum(taps[j:j + 1] * e[first + j:first + j + part, :] for j in range(3))
 
-    def spread(source, dst, ssem, rsem, blocks):
-        def send(c):
-            block = source(pl.ds(pl.multiple_of(c * part, part), part))
-
-            @pl.when(c == me_c)
-            def _():
-                local(block, dst, rsem)
-
-            @pl.when(c != me_c)
-            def _():
-                chan_copy(block, dst, ssem, rsem, c).start()
-
-        if blocks == "last":
-            send(C - 1)
-            return
+    def spread(source, dst, ssem, rsem, late):
+        def block(c):
+            return source(pl.ds(pl.multiple_of(c * part, part), part))
+
+        def fits(c):
+            return c >= 0 if late is None else (c == C - 1 if late else c < C - 1)
+
         for c in chan_order:
 
-            @pl.when(c < C - 1)
+            @pl.when(fits(c))
             def _(c=c):
-                chan_copy(source(pl.ds(pl.multiple_of(c * part, part), part)), dst, ssem, rsem, c).start()
-
-        @pl.when(me_c < C - 1)
-        def _():
-            local(source(pl.ds(pl.multiple_of(me_c * part, part), part)), dst, rsem)
+                chan_copy(block(c), dst, ssem, rsem, c).start()
+
+        @pl.when(fits(me_c))
+        def _():
+            local(block(me_c), dst, rsem)
 
     loads["cv"].wait()
     loads["st"].wait()
@@ -197,7 +195,7 @@
         for c in range(C - 1) if blocks == "first" else [C - 1]:
             wq[c * part:(c + 1) * part, :] = taps3(eq, c * part, st_ref[0]).astype(bf16)
         dst = out_ref.at[0, :, pl.ds(pl.multiple_of(me_c * channels, channels), channels)]
-        spread(lambda at: wq.at[at, :], dst, o_ssem.at[2], o_rsem.at[2], blocks)
+        spread(lambda at: wq.at[at, :], dst, o_ssem.at[2], o_rsem.at[2], blocks == "last")
 
     query("first")
 
@@ -252,7 +250,24 @@
                 acc[...] = product
             else:
                 acc[0:n * PER, :] += product
-        y_send[g] = acc[...].astype(bf16).reshape(tiles, PER, TILE)
+        result = acc[...].astype(bf16)
+        y_send[g] = result.reshape(tiles, PER, TILE)
+        pick = (
+            lax.broadcasted_iota(jnp.int32, (8, LANES), 0) == lax.broadcasted_iota(jnp.int32, (8, LANES), 1)
+        ).astype(f32).astype(bf16)
+        heads = lax.dot_general(
+            pick, result[:, 0:LANES], (((1,), (1,)), ((), ())), preferred_element_type=f32
+        )
+        place = lax.rem(me_s, LANES // PER) * PER
+        for j in range(S - 1):
+            lane = (j + 1) * own * PER
+            base = lane // LANES * LANES
+            moved = pltpu.roll(heads[:, base:base + LANES], lax.rem(place + LANES - lane % LANES, LANES), 1)
+            edge_send[g, j] = moved[0:2]
+        edge_send[g, S - 1] = jnp.zeros((2, LANES), f32)
+        local(edge_send.at[g, me_s], edge_recv.at[g, me_s], e_rsem.at[g])
+        for j in seq_order:
+            seq_copy(edge_send.at[g, j], edge_recv.at[g, me_s], e_ssem.at[g], e_rsem.at[g], j).start()
         local(y_send.at[g, pl.ds(me_s * own, own)], y_recv.at[g, me_s], y_rsem.at[g])
 
         for j in seq_order:
@@ -264,19 +279,6 @@
     wait_halo(q_src, q_dst, 0)
     query("last")
     correlate(1)
-
-    def weigh(g, blocks):
-        cols = slice(g * half, (g + 1) * half)
-        for c in range(C - 1) if blocks == "first" else [C - 1]:
-            for p in range(2):
-                wz[g, p, c * part:(c + 1) * part, :] = taps3(
-                    ez.at[g, p], c * part, st_ref[1 + p, :, cols]
-                ).astype(bf16)
-        dst = out_ref.at[1:3, :, pl.ds(pl.multiple_of(me_c * channels + g * half, half), half)]
-        spread(lambda at: wz.at[g, :, at, :], dst, o_ssem.at[g], o_rsem.at[g], blocks)
-
-    def halo_ends(g):
-        return ez.at[g, :, 0:8, :], ez.at[g, :, rows:rows + 8, :]
 
     def finish(g):
         cols = slice(g * half, (g + 1) * half)
@@ -286,16 +288,29 @@
             gz = y_recv[g, :, h].reshape(half, TILE).T.astype(f32)
             ez[g, 0, at, :] = gz * qkv_ref[2, at, cols].astype(f32)
             ez[g, 1, at, :] = gz * qkv_ref[1, at, cols].astype(f32)
-            if h == 0:
-                push_halo(*halo_ends(g), 1 + g)
-        weigh(g, "first")
-
-    loads["kv"].wait()
+        landed(edge_recv.at[g], e_rsem.at[g])
+        group = lax.broadcasted_iota(jnp.int32, (2, LANES), 1) // PER
+        per_tile = LANES // PER
+        edges = []
+        for tile in range(half // LANES):
+            edge = edge_recv[g, tile * per_tile]
+            for k in range(1, per_tile):
+                edge = jnp.where(group == k, edge_recv[g, tile * per_tile + k], edge)
+            edges.append(edge)
+        edge = jnp.concatenate(edges, 1)
+        ez[g, 0, rows:rows + 2, :] = edge * kv_edge[1, :, cols].astype(f32)[0:2]
+        ez[g, 1, rows:rows + 2, :] = edge * kv_edge[0, :, cols].astype(f32)[0:2]
+        for c in range(C):
+            for p in range(2):
+                wz[g, p, c * part:(c + 1) * part, :] = taps3(
+                    ez.at[g, p], c * part, st_ref[1 + p, :, cols]
+                ).astype(bf16)
+        dst = out_ref.at[1:3, :, pl.ds(pl.multiple_of(me_c * channels + g * half, half), half)]
+        spread(lambda at: wz.at[g, :, at, :], dst, o_ssem.at[g], o_rsem.at[g], None)
+
+    kv_copy.wait_recv()
     finish(0)
     finish(1)
-    for g in range(2):
-        wait_halo(*halo_ends(g), 1 + g)
-        weigh(g, "last")
 
     landed(out_ref.at[0], o_rsem.at[2])
     for g in range(2):
@@ -304,11 +319,12 @@
     landed(tap_send.at[0:S - 1], tap_sem.at[0])
     landed(wq.at[0:rows - part, :], o_ssem.at[2])
     wait_halo_sent(q_src, q_dst, 0)
+    kv_copy.wait_send()
     for g in range(2):
         landed(x_send.at[g, 0:S - 1], x_ssem.at[g])
         landed(y_send.at[g, 0:tiles - own], y_ssem.at[g])
         landed(wz.at[g, :, 0:rows - part, :], o_ssem.at[g])
-        wait_halo_sent(*halo_ends(g), 1 + g)
+        landed(edge_send.at[g, 0:S - 1], e_ssem.at[g])
 
 
 def on_device(S, C, grad_out, qkv_saved, conv_saved, long_taps, short_taps):
@@ -338,6 +354,9 @@
             pltpu.VMEM((tiles * PER, TILE), f32),
             pltpu.VMEM((2, tiles, PER, TILE), bf16),
             pltpu.VMEM((2, S, own, PER, TILE), bf16),
+            pltpu.VMEM((2, S, 2, LANES), f32),
+            pltpu.VMEM((2, S, 2, LANES), f32),
+            pltpu.VMEM((2, PER, channels), bf16),
             pltpu.VMEM((rows + 8, channels), f32),
             pltpu.VMEM((2, 2, rows + 8, half), f32),
             pltpu.VMEM((rows, channels), bf16),
@@ -347,8 +366,10 @@
             pltpu.SemaphoreType.DMA((2,)),
             pltpu.SemaphoreType.DMA((2,)),
             pltpu.SemaphoreType.DMA((2,)),
-            pltpu.SemaphoreType.DMA((3,)),
-            pltpu.SemaphoreType.DMA((3,)),
+            pltpu.SemaphoreType.DMA((2,)),
+            pltpu.SemaphoreType.DMA((2,)),
+            pltpu.SemaphoreType.DMA((2,)),
+            pltpu.SemaphoreType.DMA((2,)),
             pltpu.SemaphoreType.DMA((3,)),
             pltpu.SemaphoreType.DMA((3,)),
         ],

time: 51.3 us -> 48.8 us (0.951)
  the two profiles are of different devices: /device:TPU:30 before, /device:TPU:1 now
where the time goes in v3:
time: 48.8 us; the launch traced here: 48.7 us
  Pallas kernels  47.5 us (97%)
  local copies, waits for them, and re-layouts  1.15 us (2%)
    pallas_call x1, Pallas kernels, on_device(): pl.pallas_call(functools.partial(kernel, S, C), out_shape=jax.ShapeDtypeS...  47.5 us
    unnamed x1, local copies, waits for them, and re-layouts  1.15 us

profile of v3, /device:TPU:1, one launch (start us, length us, event | category | flops | bytes accessed | tf_op | source)
XLA Modules:
  0.0 48.7 jit_solution(5110942153949463338)
XLA Ops:
  0.0 47.5 %shard_map.55 = bf16[3,32,8192]{2,1,0:T(8,128)(2,1)S(1)} custom-call(bf16[512,512]{1,0:T(8,128)(2,1)} %go_hbm.1, bf16[3,512,512]{2,1,0:T(8,128)(2,1)} %bitcast.4, bf16[512,512]{1,0:T(8,128)(2,1)} %cv_hbm.1, bf16[32,512]{1,0:T(8,128)(2,1)} %bitcast.5, f32[3,3,512]{2,1,0:T(4,128)} %st_hbm.1), custom_call_target="tpu_custom_call" | custom-call | tf_op jit(solution)/shard_map/pallas_call | solution.py:336
  47.5 1.1 %copy.7 = bf16[32,3,8192]{2,0,1:T(8,128)(2,1)} copy(bf16[32,3,8192]{2,0,1:T(8,128)(2,1)S(1)} %bitcast.3) | data formatting | bytes 3145728

commit v4 on v3

v4 whole, which is shorter than its diff:
```python
import functools
import math

import jax
import jax.numpy as jnp
from jax import lax
from jax.experimental import pallas as pl
from jax.experimental.pallas import tpu as pltpu
from jax.sharding import PartitionSpec as P

MESH = pl.DeviceIdType.MESH
f32 = jnp.float32
bf16 = jnp.bfloat16

LANES = 128
TILE = 256
PER = 16
FEW = 8
PIECES = 4
SEG = 8


def kernel(
    S, C,
    go_hbm, qkv_hbm, cv_hbm, tp_hbm, st_hbm, out_ref,
    go_ref, qkv_ref, cv_ref, tp_ref, st_ref, in_sem,
    tap_rows, tap_send, tap_recv, rev_ref, strip, x_send, x_recv, x_wide, acc, y_send, y_recv,
    edge_send, edge_recv, near_send, near_recv, eq, ez, wq, wz,
    tap_sem, x_ssem, x_rsem, y_ssem, y_rsem, e_ssem, e_rsem, h_ssem, h_rsem, o_ssem, o_rsem,
):
    rows, channels = go_ref.shape
    half = channels // 2
    piece = channels // PIECES
    tiles = S * rows // TILE
    own = rows // TILE
    part = rows // C
    me_s = lax.axis_index("seq")
    me_c = lax.axis_index("chan")

    def local(src, dst, sem):
        pltpu.make_async_copy(src, dst, sem).start()

    def landed(ref, sem):
        pltpu.make_async_copy(ref, ref, sem).wait()

    def seq_copy(src, dst, ssem, rsem, j):
        return pltpu.make_async_remote_copy(
            src_ref=src, dst_ref=dst, send_sem=ssem, recv_sem=rsem,
            device_id=(j, me_c), device_id_type=MESH,
        )

    def chan_copy(src, dst, ssem, rsem, j):
        return pltpu.make_async_remote_copy(
            src_ref=src, dst_ref=dst, send_sem=ssem, recv_sem=rsem,
            device_id=(me_s, j), device_id_type=MESH,
        )

    turn = 1 - 2 * lax.rem(me_s, 2)
    if S % 2 == 0:
        chips = S // 2
        steps = sorted(range(1, chips), key=lambda z: -min(z, chips - z))
        seq_order = [
            lax.rem(me_s // 2 + turn * z + chips, chips) * 2 + lax.rem(me_s + core, 2) for z in steps for core in range(2)
        ] + [me_s + turn]
    else:
        seq_order = [lax.rem(me_s + k, S) for k in range(1, S)]
    side = math.isqrt(C)
    if side * side == C:
        moves = sorted(
            [(x, y) for x in range(side) for y in range(side) if x + y > 0],
            key=lambda m: -(min(m[0], side - m[0]) + min(m[1], side - m[1])),
        )
        chan_order = [
            lax.rem(me_c // side + turn * x + side, side) * side + lax.rem(lax.rem(me_c, side) + turn * y + side, side)
            for x, y in moves
        ]
    else:
        chan_order = [lax.rem(me_c + k, C) for k in range(1, C)]

    barrier = pltpu.get_barrier_semaphore()

    def greet_seq(k, carry):
        pl.semaphore_signal(barrier, inc=1, device_id=(lax.rem(me_s + k, S), me_c), device_id_type=MESH)
        return carry

    def greet_chan(k, carry):
        pl.semaphore_signal(barrier, inc=1, device_id=(me_s, lax.rem(me_c + k, C)), device_id_type=MESH)
        return carry

    lax.fori_loop(1, S, greet_seq, 0)
    lax.fori_loop(1, C, greet_chan, 0)

    loads = {}

    def load(name, src, dst):
        loads[name] = pltpu.make_async_copy(src, dst, in_sem.at[len(loads)])
        loads[name].start()

    load("tp", tp_hbm, tp_ref)
    for g in range(2):
        cols = slice(g * half, (g + 1) * half)
        load(f"go{g}", go_hbm.at[:, cols], go_ref.at[:, cols])
        load(f"q{g}", qkv_hbm.at[0, :, cols], qkv_ref.at[0, :, cols])
    load("cv", cv_hbm, cv_ref)
    load("st", st_hbm, st_ref)
    load("kv", qkv_hbm.at[1:3], qkv_ref.at[1:3])

    quarters = rows // LANES
    loads["tp"].wait()
    for u in range(PIECES):
        for q in range(quarters):
            chunk = tp_ref[u * (S // 2):(u + 1) * (S // 2), q * LANES:(q + 1) * LANES].astype(f32)
            tap_rows[:, u * quarters + q, :] = chunk
    tap_send[...] = tap_rows[...].astype(bf16)

    def mix(g):
        cols = slice(g * half, (g + 1) * half)
        loads[f"go{g}"].wait()
        loads[f"q{g}"].wait()
        turned = (go_ref[:, cols].astype(f32) * qkv_ref[0, :, cols].astype(f32)).T.reshape(2, S, FEW, rows)
        paired = jnp.concatenate([turned[0], turned[1]], 1).astype(bf16)
        for h in range(own):
            x_send[g, :, h] = paired[:, :, h * TILE:(h + 1) * TILE]

    pl.semaphore_wait(barrier, S + C - 2)

    local(tap_send.at[me_s // 2], tap_recv.at[me_s], tap_sem.at[1])

    for j in seq_order:
        seq_copy(tap_send.at[j // 2], tap_recv.at[me_s], tap_sem.at[0], tap_sem.at[1], j).start()

    mix(0)

    def push_x(g):
        mine = pl.ds(me_s * own, own)
        local(x_send.at[g, me_s], x_recv.at[g, mine], x_rsem.at[g])

        for j in seq_order:
            seq_copy(x_send.at[g, j], x_recv.at[g, mine], x_ssem.at[g], x_rsem.at[g], j).start()

    push_x(0)
    mix(1)
    push_x(1)

    loads["kv"].wait()
    loads["cv"].wait()
    loads["st"].wait()
    head = slice(0, PER)
    near_send[0] = (go_ref[head].astype(f32) * cv_ref[head].astype(f32))[0:2]
    for p in range(1, 3):
        near_send[p] = qkv_ref[p, head].astype(f32)[0:2]
    near = seq_copy(near_send, near_recv, h_ssem.at[0], h_rsem.at[0], lax.rem(me_s + S - 1, S))
    near.start()

    def taps3(e, first, taps):
        return sum(taps[j:j + 1] * e[first + j:first + j + part, :] for j in range(3))

    def spread(source, dst, ssem, rsem, late):
        def block(c):
            return source(pl.ds(pl.multiple_of(c * part, part), part))

        def fits(c):
            return c >= 0 if late is None else (c == C - 1 if late else c < C - 1)

        for c in chan_order:

            @pl.when(fits(c))
            def _(c=c):
                chan_copy(block(c), dst, ssem, rsem, c).start()

        @pl.when(fits(me_c))
        def _():
            local(block(me_c), dst, rsem)

    eq[0:rows, :] = go_ref[...].astype(f32) * cv_ref[...].astype(f32)

    def query(blocks):
        for c in range(C - 1) if blocks == "first" else [C - 1]:
            wq[c * part:(c + 1) * part, :] = taps3(eq, c * part, st_ref[0]).astype(bf16)
        dst = out_ref.at[0, :, pl.ds(pl.multiple_of(me_c * channels, channels), channels)]
        spread(lambda at: wq.at[at, :], dst, o_ssem.at[PIECES], o_rsem.at[PIECES], blocks == "last")


    landed(tap_recv, tap_sem.at[1])
    down = lax.broadcasted_iota(jnp.int32, (LANES, LANES), 0)
    over = lax.broadcasted_iota(jnp.int32, (LANES, LANES), 1)
    mirror = (lax.rem(down + over, LANES) == 0).astype(f32).astype(bf16)
    rev = jnp.dot(
        tap_recv[...].reshape(S * PIECES * quarters, LANES), mirror, preferred_element_type=f32
    )
    rev_ref[...] = rev.reshape(S, PIECES, quarters, LANES)
    newer = (over == 0) | (over >= LANES - down)

    strip[:, 0:LANES, :] = jnp.zeros((PIECES, LANES, LANES), bf16)

    def build(pieces):
        def grow(s, before):
            after = []
            for u, last in zip(pieces, before):
                for q in range(quarters):
                    row = rev_ref[s, u, q:q + 1, :]
                    mixed = jnp.where(
                        newer, jnp.broadcast_to(row, (LANES, LANES)), jnp.broadcast_to(last, (LANES, LANES))
                    )
                    rolled = pltpu.roll(mixed, 0, 1, stride=1, stride_axis=0)
                    at = pl.multiple_of((s * quarters + q + 1) * LANES, LANES)
                    strip[u, pl.ds(at, LANES), :] = rolled.astype(bf16)
                    last = row
                after.append(last)
            return tuple(after)

        nothing = jnp.zeros((1, LANES), f32)
        lax.fori_loop(0, S, grow, (nothing,) * len(pieces))

    x_wide[:, tiles:tiles + SEG - 1] = jnp.zeros((2, SEG - 1, FEW, TILE), f32)

    def widen(g):
        landed(x_recv.at[g, 0:tiles], x_rsem.at[g])
        wide = x_recv[g, 0:tiles].astype(f32)
        for side_of in range(2):
            x_wide[side_of, 0:tiles] = wide[:, side_of * FEW:(side_of + 1) * FEW]

    pick = (
        lax.broadcasted_iota(jnp.int32, (8, LANES), 0) == lax.broadcasted_iota(jnp.int32, (8, LANES), 1)
    ).astype(f32).astype(bf16)

    def correlate(u):
        g, side_of = u // 2, u % 2
        for seg in range(tiles // SEG):
            n = tiles - seg * SEG
            deep = SEG * TILE
            left = jnp.concatenate(
                [x_wide[side_of, seg * SEG + d:seg * SEG + d + n].reshape(n * FEW, TILE) for d in range(SEG)], 1
            ).astype(bf16)
            right = jnp.concatenate(
                [
                    strip[u, LANES + seg * deep:LANES + (seg + 1) * deep, :],
                    strip[u, seg * deep:(seg + 1) * deep, :],
                ],
                1,
            )
            product = jnp.dot(left, right, preferred_element_type=f32)
            if seg == 0:
                acc[...] = product
            else:
                acc[0:n * FEW, :] += product
        result = acc[...].reshape(S, own * FEW, TILE).astype(bf16)
        y_send[u] = result
        local(y_send.at[u, me_s], y_recv.at[u, me_s], y_rsem.at[u])
        for j in seq_order:
            seq_copy(y_send.at[u, j], y_recv.at[u, me_s], y_ssem.at[u], y_rsem.at[u], j).start()

    def edges(g):
        heads = [
            lax.dot_general(
                pick, y_send[2 * g + a, :, :, 0:LANES].reshape(S * own * FEW, LANES), (((1,), (1,)), ((), ())),
                preferred_element_type=f32,
            )
            for a in range(2)
        ]
        second = lax.broadcasted_iota(jnp.int32, (8, LANES), 1) // FEW == lax.rem(me_s + S // 2, S)
        for j in range(S - 1):
            lane = (j + 1) * own * FEW
            base = lane // LANES * LANES
            moved = [
                pltpu.roll(
                    heads[a][:, base:base + LANES],
                    lax.rem(me_s * FEW + a * (LANES // 2) + LANES - lane % LANES, LANES), 1,
                )
                for a in range(2)
            ]
            edge_send[g, j] = jnp.where(second, moved[1], moved[0])[0:2]
        edge_send[g, S - 1] = jnp.zeros((2, LANES), f32)
        local(edge_send.at[g, me_s], edge_recv.at[g, me_s], e_rsem.at[g])
        for j in seq_order:
            seq_copy(edge_send.at[g, j], edge_recv.at[g, me_s], e_ssem.at[g], e_rsem.at[g], j).start()

    build((0, 1))
    build((2, 3))
    widen(0)
    correlate(0)
    correlate(1)
    edges(0)
    near.wait_recv()
    eq[rows:rows + 2, :] = jnp.where(me_s == S - 1, 0.0, near_recv[0])
    query("first")
    query("last")
    widen(1)
    correlate(2)
    correlate(3)
    edges(1)

    def finish(u):
        cols = slice(u * piece, (u + 1) * piece)
        landed(y_recv.at[u], y_rsem.at[u])
        wide = y_recv[u].astype(f32)
        for h in range(own):
            at = slice(h * TILE, (h + 1) * TILE)
            gz = wide[:, h * FEW:(h + 1) * FEW].reshape(piece, TILE).T
            ez[u, 0, at, :] = gz * qkv_ref[2, at, cols].astype(f32)
            ez[u, 1, at, :] = gz * qkv_ref[1, at, cols].astype(f32)
        g, a = u // 2, u % 2
        if a == 0:
            landed(edge_recv.at[g], e_rsem.at[g])
        source = lax.broadcasted_iota(jnp.int32, (2, LANES), 1) // FEW
        edge = edge_recv[g, 0]
        for k in range(1, S):
            edge = jnp.where(source == (k + a * (S // 2)) % S, edge_recv[g, k], edge)
        if a == 1:
            edge = jnp.concatenate([edge[:, LANES // 2:], edge[:, 0:LANES // 2]], 1)
        ez[u, 0, rows:rows + 2, :] = edge * near_recv[2, :, cols]
        ez[u, 1, rows:rows + 2, :] = edge * near_recv[1, :, cols]
        for c in range(C):
            for p in range(2):
                wz[u, p, c * part:(c + 1) * part, :] = taps3(
                    ez.at[u, p], c * part, st_ref[1 + p, :, cols]
                ).astype(bf16)
        dst = out_ref.at[1:3, :, pl.ds(pl.multiple_of(me_c * channels + u * piece, piece), piece)]
        spread(lambda at: wz.at[u, :, at, :], dst, o_ssem.at[u], o_rsem.at[u], None)

    for u in range(PIECES):
        finish(u)

    landed(out_ref.at[0], o_rsem.at[PIECES])
    for u in range(PIECES):
        landed(out_ref.at[1:3, :, 0:C * piece], o_rsem.at[u])

    landed(tap_recv.at[0:S - 1], tap_sem.at[0])
    landed(wq.at[0:rows - part, :], o_ssem.at[PIECES])
    near.wait_send()
    for g in range(2):
        landed(x_send.at[g, 0:S - 1], x_ssem.at[g])
        landed(edge_send.at[g, 0:S - 1], e_ssem.at[g])
    for u in range(PIECES):
        landed(y_send.at[u, 0:S - 1], y_ssem.at[u])
        landed(wz.at[u, :, 0:rows - part, :], o_ssem.at[u])


def on_device(S, C, grad_out, qkv_saved, conv_saved, long_taps, short_taps):
    rows, channels = grad_out.shape
    piece = channels // PIECES
    tiles = S * rows // TILE
    own = rows // TILE
    quarters = rows // LANES
    out = pl.pallas_call(
        functools.partial(kernel, S, C),
        out_shape=jax.ShapeDtypeStruct((3, rows // C, C * channels), bf16),
        in_specs=[pl.BlockSpec(memory_space=pltpu.HBM)] * 5,
        out_specs=pl.BlockSpec(memory_space=pl.ANY),
        scratch_shapes=[
            pltpu.VMEM((rows, channels), bf16),
            pltpu.VMEM((3, rows, channels), bf16),
            pltpu.VMEM((rows, channels), bf16),
            pltpu.VMEM((2 * S, rows), bf16),
            pltpu.VMEM((3, 3, channels), f32),
            pltpu.SemaphoreType.DMA((8,)),
            pltpu.VMEM((S // 2, PIECES * quarters, LANES), f32),
            pltpu.VMEM((S // 2, PIECES * quarters, LANES), bf16),
            pltpu.VMEM((S, PIECES * quarters, LANES), bf16),
            pltpu.VMEM((S, PIECES, quarters, LANES), f32),
            pltpu.VMEM((PIECES, LANES + tiles * TILE, LANES), bf16),
            pltpu.VMEM((2, S, own, PER, TILE), bf16),
            pltpu.VMEM((2, tiles + SEG, PER, TILE), bf16),
            pltpu.VMEM((2, tiles + SEG, FEW, TILE), f32),
            pltpu.VMEM((tiles * FEW, TILE), f32),
            pltpu.VMEM((PIECES, S, own * FEW, TILE), bf16),
            pltpu.VMEM((PIECES, S, own * FEW, TILE), bf16),
            pltpu.VMEM((2, S, 2, LANES), f32),
            pltpu.VMEM((2, S, 2, LANES), f32),
            pltpu.VMEM((3, 2, channels), f32),
            pltpu.VMEM((3, 2, channels), f32),
            pltpu.VMEM((rows + 8, channels), f32),
            pltpu.VMEM((PIECES, 2, rows + 8, piece), f32),
            pltpu.VMEM((rows, channels), bf16),
            pltpu.VMEM((PIECES, 2, rows, piece), bf16),
            pltpu.SemaphoreType.DMA((2,)),
            pltpu.SemaphoreType.DMA((2,)),
            pltpu.SemaphoreType.DMA((2,)),
            pltpu.SemaphoreType.DMA((PIECES,)),
            pltpu.SemaphoreType.DMA((PIECES,)),
            pltpu.SemaphoreType.DMA((PIECES,)),
            pltpu.SemaphoreType.DMA((PIECES,)),
            pltpu.SemaphoreType.DMA((2,)),
            pltpu.SemaphoreType.DMA((2,)),
            pltpu.SemaphoreType.DMA((PIECES + 1,)),
            pltpu.SemaphoreType.DMA((PIECES + 1,)),
        ],
        compiler_params=pltpu.CompilerParams(
            collective_id=0, has_side_effects=True, vmem_limit_bytes=48 * 1024 * 1024
        ),
    )(*[
        pltpu.with_memory_space_constraint(value, pltpu.HBM)
        for value in (grad_out, qkv_saved.transpose(1, 0, 2), conv_saved, long_taps.T, short_taps)
    ])
    return out.transpose(1, 0, 2)


def solution(mesh):
    in_specs = (
        P("seq", "chan"),
        P("seq", None, "chan"),
        P("seq", "chan"),
        P("seq", "chan"),
        P(None, None, "chan"),
    )
    out_specs = P(("seq", "chan"), None, None)
    return jax.shard_map(
        functools.partial(on_device, mesh.shape["seq"], mesh.shape["chan"]),
        mesh=mesh, in_specs=in_specs, out_specs=out_specs, check_vma=False,
    )
```

time: 48.8 us -> 48.7 us (level)
  no operation moved by 1% of the time
where the time goes in v4:
time: 48.7 us; the launch traced here: 48.6 us
  Pallas kernels  47.4 us (97%)
  local copies, waits for them, and re-layouts  1.15 us (2%)
    pallas_call x1, Pallas kernels, on_device(): pl.pallas_call(functools.partial(kernel, S, C), out_shape=jax.ShapeDtypeS...  47.4 us
    unnamed x1, local copies, waits for them, and re-layouts  1.15 us

profile of v4, /device:TPU:1, one launch (start us, length us, event | category | flops | bytes accessed | tf_op | source)
XLA Modules:
  0.0 48.6 jit_solution(12555885697573097154)
XLA Ops:
  0.0 47.4 %shard_map.55 = bf16[3,32,8192]{2,1,0:T(8,128)(2,1)S(1)} custom-call(bf16[512,512]{1,0:T(8,128)(2,1)} %go_hbm.1, bf16[3,512,512]{2,1,0:T(8,128)(2,1)} %bitcast.4, bf16[512,512]{1,0:T(8,128)(2,1)} %cv_hbm.1, bf16[32,512]{1,0:T(8,128)(2,1)} %bitcast.5, f32[3,3,512]{2,1,0:T(4,128)} %st_hbm.1), custom_call_target="tpu_custom_call" | custom-call | tf_op jit(solution)/shard_map/pallas_call | solution.py:345
  47.4 1.1 %copy.7 = bf16[32,3,8192]{2,0,1:T(8,128)(2,1)} copy(bf16[32,3,8192]{2,0,1:T(8,128)(2,1)S(1)} %bitcast.3) | data formatting | bytes 3145728

commit v5 on v4

--- a/solution.py
+++ b/solution.py
@@ -56,14 +56,8 @@
         )
 
     turn = 1 - 2 * lax.rem(me_s, 2)
-    if S % 2 == 0:
-        chips = S // 2
-        steps = sorted(range(1, chips), key=lambda z: -min(z, chips - z))
-        seq_order = [
-            lax.rem(me_s // 2 + turn * z + chips, chips) * 2 + lax.rem(me_s + core, 2) for z in steps for core in range(2)
-        ] + [me_s + turn]
-    else:
-        seq_order = [lax.rem(me_s + k, S) for k in range(1, S)]
+    steps = sorted(range(1, S), key=lambda k: -min(k, S - k))
+    seq_order = [lax.rem(me_s + k, S) for k in steps]
     side = math.isqrt(C)
     if side * side == C:
         moves = sorted(

time: 48.7 us -> 49 us (level)
  no operation moved by 1% of the time
where the time goes in v5:
time: 49 us; the launch traced here: 48.9 us
  Pallas kernels  47.7 us (97%)
  local copies, waits for them, and re-layouts  1.15 us (2%)
    pallas_call x1, Pallas kernels, on_device(): pl.pallas_call(functools.partial(kernel, S, C), out_shape=jax.ShapeDtypeS...  47.7 us
    unnamed x1, local copies, waits for them, and re-layouts  1.15 us

profile of v5, /device:TPU:1, one launch (start us, length us, event | category | flops | bytes accessed | tf_op | source)
XLA Modules:
  0.0 48.9 jit_solution(5870383004697423883)
XLA Ops:
  0.0 47.7 %shard_map.55 = bf16[3,32,8192]{2,1,0:T(8,128)(2,1)S(1)} custom-call(bf16[512,512]{1,0:T(8,128)(2,1)} %go_hbm.1, bf16[3,512,512]{2,1,0:T(8,128)(2,1)} %bitcast.4, bf16[512,512]{1,0:T(8,128)(2,1)} %cv_hbm.1, bf16[32,512]{1,0:T(8,128)(2,1)} %bitcast.5, f32[3,3,512]{2,1,0:T(4,128)} %st_hbm.1), custom_call_target="tpu_custom_call" | custom-call | tf_op jit(solution)/shard_map/pallas_call | solution.py:339
  47.7 1.1 %copy.7 = bf16[32,3,8192]{2,0,1:T(8,128)(2,1)} copy(bf16[32,3,8192]{2,0,1:T(8,128)(2,1)S(1)} %bitcast.3) | data formatting | bytes 3145728
